TPU v7x, 32 devices: a whole 2x2x4 slice. The times are simulated.
32 devices in a mesh: pts: 8 (over z, y), ch: 4 (over x, core).
Axes of the slice: x: 2, y: 2, z: 4, core: 2. Of those that a mesh axis runs over, the one named last changes fastest.
Arguments:
- points_in: bfloat16 [4096, 256], P('pts'), may hold values from -6 to 6
- neighbor_offsets: int32 [4096, 16], P('pts'), may hold values from -128 to 128, as said below
- kernel_ids: int32 [4096, 16], P('pts'), may hold values from 0 to 26
- cluster_ids: int32 [4096], P('pts'), may hold values from 0 to 1023, as said below
- owners: int32 [4096], P('pts'), may hold values from 0 to 7, as said below
- conv_weight: bfloat16 [27, 256], replicated, may hold values from -1.5 to 1.5
- norm_gain: float32 [256], replicated, may hold values from 0.1 to 1.9
- norm_bias: float32 [256], replicated, may hold values from -3 to 3
- qkv_weight: bfloat16 [3, 256, 256], P(None, None, 'ch'), may hold values from -20 to 20
- proj_weight: bfloat16 [256, 256], replicated, may hold values from -1.5 to 1.5
- pool_weight: bfloat16 [256, 512], P(None, 'ch'), may hold values from -0.375 to 0.375
Outputs:
- block_out: bfloat16 [4096, 256], P('pts', 'ch')
- pooled: bfloat16 [1024, 512], P('pts', 'ch')
Inputs may be any that keep to these rules, and one draw needn't show every extreme that they name: `owners`: each device's points name every owner at most 128 times; in every draw one owner is named exactly 128 times by the points of every device. `cluster_ids`: cluster ids never fall along the points, every cluster holds one or more points, the points of device i belong to clusters i * 128 - 1 .. i * 128 + 127, and only the first 1 to 3 points of a device (none on device 0) lie in cluster i * 128 - 1; some device has exactly 3 such points. `neighbor_offsets`: offsets -128 and 128 both occur.
All inputs are finite; a program needn't handle non-finite values.
Results may differ from a plain program's by a relative error of at most 0.017.
Values may be sent and summed in bfloat16 or wider, within the bound.
A program may use at most 64 MiB of HBM per device.

v0:
```python
import functools
import math

import jax
import jax.numpy as jnp
from jax import lax
from jax.experimental import pallas as pl
from jax.experimental.pallas import tpu as pltpu
from jax.sharding import PartitionSpec as P

HD = 32
G = 128
TILE = 128
CHUNK = 4
QTILE = 256
MESH = pl.DeviceIdType.MESH
BF = jnp.bfloat16
F32 = jnp.float32


def iota(shape, dim):
    return lax.broadcasted_iota(jnp.int32, shape, dim)


def dot(a, b):
    return jnp.dot(a, b, preferred_element_type=F32)


def kernel(
    nodes,
    chans,
    cap,
    x_ref,
    off_ref,
    kid_ref,
    cid_ref,
    own_ref,
    cw_ref,
    gain_ref,
    bias_ref,
    qkvw_ref,
    proj_ref,
    pool_ref,
    full_ref,
    mean_ref,
    xp,
    cw,
    res,
    ext,
    send,
    recv,
    back,
    ret,
    pack,
    gath,
    pw,
    spill_out,
    spill_in,
    halo_send,
    halo_recv,
    fwd_send,
    fwd_recv,
    ret_send,
    ret_recv,
    ch_send,
    ch_recv,
    sp_send,
    sp_recv,
):
    me = lax.axis_index("pts")
    ch = lax.axis_index("ch")
    rows, feats = x_ref.shape
    half = cap // 2
    slots = nodes * cap

    barrier = pltpu.get_barrier_semaphore()

    @pl.loop(1, nodes)
    def _(r):
        pl.semaphore_signal(
            barrier, inc=1, device_id={"pts": lax.rem(me + r, nodes)}, device_id_type=MESH
        )

    for r in range(1, chans):
        pl.semaphore_signal(
            barrier, inc=1, device_id={"ch": lax.rem(ch + r, chans)}, device_id_type=MESH
        )
    pl.semaphore_wait(barrier, nodes - 1 + chans - 1)

    def halo_copy(up):
        if up:
            src, dst, to, at = x_ref.at[pl.ds(rows - G, G)], xp.at[pl.ds(0, G)], me + 1, 0
        else:
            src, dst, to, at = x_ref.at[pl.ds(0, G)], xp.at[pl.ds(rows + G, G)], me - 1, 1
        return pltpu.make_async_remote_copy(
            src_ref=src,
            dst_ref=dst,
            send_sem=halo_send.at[at],
            recv_sem=halo_recv.at[at],
            device_id={"pts": to},
            device_id_type=MESH,
        )

    @pl.when(me < nodes - 1)
    def _():
        halo_copy(True).start()

    @pl.when(me > 0)
    def _():
        halo_copy(False).start()

    @pl.when(me == 0)
    def _():
        xp[pl.ds(0, G), :] = jnp.zeros((G, feats), BF)

    @pl.when(me == nodes - 1)
    def _():
        xp[pl.ds(rows + G, G), :] = jnp.zeros((G, feats), BF)

    xp[pl.ds(G, rows), :] = x_ref[...]
    kinds = cw_ref.shape[0]
    cw[...] = jnp.zeros_like(cw)
    cw[pl.ds(0, kinds), :] = cw_ref[...]

    head_cols = feats // chans
    pw[...] = jnp.zeros_like(pw)
    for c in range(chans):
        part = proj_ref[pl.ds(c * head_cols, head_cols), :]
        pw[0, pl.ds(2 * c * head_cols, head_cols), :] = part
        pw[1, pl.ds((2 * c + 1) * head_cols, head_cols), :] = part

    owner_row = own_ref[...]
    owner_rows = max(nodes, 16)
    marks = iota((owner_rows, rows), 0) == owner_row
    before = (iota((rows, rows), 0) < iota((rows, rows), 1)).astype(F32).astype(BF)
    earlier = dot(marks.astype(F32).astype(BF), before)
    slot_row = jnp.sum(jnp.where(marks, earlier, 0.0), axis=0, keepdims=True).astype(jnp.int32)
    pos_row = owner_row * cap + slot_row
    upper = (slot_row >= half).astype(jnp.int32)
    ret_row = owner_row * half + slot_row - upper * half
    ret_col = jnp.transpose(jnp.broadcast_to(ret_row, (128, rows)).astype(F32)).astype(jnp.int32)
    up_col = jnp.transpose(jnp.broadcast_to(upper, (128, rows)).astype(F32)).astype(jnp.int32)

    gain = gain_ref[...]
    beta = bias_ref[...]
    wqkv = jnp.concatenate(
        [
            qkvw_ref[1],
            jnp.zeros((feats, head_cols), BF),
            qkvw_ref[0],
            qkvw_ref[2],
        ],
        axis=1,
    )
    ones_lane = jnp.logical_and(
        iota((TILE, 4 * head_cols), 1) >= head_cols, iota((TILE, 4 * head_cols), 1) < 2 * head_cols
    )

    def tile(t):
        base = t * TILE
        window = xp[pl.ds(base, TILE + 2 * G), :]
        weights = cw[...]
        offs = off_ref[pl.ds(base, TILE), :] + iota((TILE, off_ref.shape[1]), 0) + G
        kids = kid_ref[pl.ds(base, TILE), :]
        lanes = iota((TILE, TILE + 2 * G), 1)
        kind_lanes = iota((TILE, 128), 1)
        conv = x_ref[pl.ds(base, TILE), :].astype(F32)
        total = jnp.zeros((TILE, feats), F32)
        for first in range(0, off_ref.shape[1], CHUNK):
            pick = jnp.concatenate(
                [
                    (lanes == offs[:, n : n + 1]).astype(F32).astype(BF)
                    for n in range(first, first + CHUNK)
                ],
                axis=0,
            )
            kind = jnp.concatenate(
                [
                    (kind_lanes == kids[:, n : n + 1]).astype(F32).astype(BF)
                    for n in range(first, first + CHUNK)
                ],
                axis=0,
            )
            product = dot(pick, window) * dot(kind, weights)
            for n in range(CHUNK):
                total = total + product[n * TILE : (n + 1) * TILE]
        residual = (conv + total).astype(BF)
        res[pl.ds(base, TILE), :] = residual
        features = residual.astype(F32)
        average = jnp.mean(features, axis=1, keepdims=True)
        centered = features - average
        variance = jnp.mean(centered * centered, axis=1, keepdims=True)
        normed = (centered * lax.rsqrt(variance + 1e-05) * gain + beta).astype(BF)
        projected = jnp.where(ones_lane, 1.0, dot(normed, wqkv))
        ext[pl.ds(base, TILE), :] = projected.astype(BF)

    tiles = rows // TILE
    for t in range(1, tiles - 1):
        tile(t)

    @pl.when(me > 0)
    def _():
        halo_copy(True).wait_recv()

    tile(0)

    @pl.when(me < nodes - 1)
    def _():
        halo_copy(False).wait_recv()

    tile(tiles - 1)

    rows_each = min(slots, 1024)
    for first in range(0, slots, rows_each):
        place = (iota((rows_each, rows), 0) + first == pos_row).astype(F32).astype(BF)
        placed = dot(place, ext[...]).astype(BF)
        send[pl.ds(first // cap, rows_each // cap)] = placed.reshape(rows_each // cap, cap, feats)

    def fwd_copy(r, to):
        return pltpu.make_async_remote_copy(
            src_ref=send.at[to],
            dst_ref=recv.at[me],
            send_sem=fwd_send.at[r],
            recv_sem=fwd_recv.at[r],
            device_id={"pts": to},
            device_id_type=MESH,
        )

    @pl.loop(1, nodes)
    def _(r):
        fwd_copy(r, lax.rem(me + r, nodes)).start()

    recv[me] = send[me]

    @pl.loop(1, nodes)
    def _(r):
        fwd_copy(r, lax.rem(me + r, nodes)).wait_recv()

    everything = recv[...].reshape(slots, feats)
    low = everything[:, : 2 * head_cols]
    lane = iota((slots, 2 * head_cols), 1)
    keys = jnp.where(
        lane < head_cols, low.astype(F32), (low.astype(F32) - 1.0) * 1e30
    ).astype(BF)
    scale = 1.0 / math.sqrt(HD)
    nodes_each = QTILE // cap
    for first in range(0, slots, QTILE):
        query = recv[pl.ds(first // cap, nodes_each)].reshape(QTILE, feats)[:, 2 * head_cols :]
        query = query.astype(F32)
        lane_q = iota((QTILE, 2 * head_cols), 1)
        answer = jnp.zeros((QTILE, 2 * head_cols), F32)
        for h in range(head_cols // HD):
            inside = jnp.logical_and(lane_q >= h * HD, lane_q < (h + 1) * HD)
            one = jnp.where(lane_q == head_cols, 1.0, 0.0)
            query_h = jnp.where(inside, query, one).astype(BF)
            scores = lax.dot_general(
                query_h, keys, (((1,), (1,)), ((), ())), preferred_element_type=F32
            )
            top = jnp.max(scores, axis=1, keepdims=True)
            soft = jnp.exp((scores - top) * scale).astype(BF)
            summed = dot(soft, everything)
            below = summed[:, head_cols : head_cols + 1]
            below = jnp.where(below == 0.0, 1.0, below)
            here = jnp.logical_and(
                lane_q >= head_cols + h * HD, lane_q < head_cols + (h + 1) * HD
            )
            answer = jnp.where(here, summed[:, 2 * head_cols :] / below, answer)
        cube = answer.reshape(nodes_each, cap, 2 * head_cols)
        moved = pltpu.roll(answer, head_cols, 1).reshape(nodes_each, cap, 2 * head_cols)
        lane_b = iota((nodes_each, half, 2 * head_cols), 2)
        both = jnp.where(lane_b < head_cols, moved[:, :half], cube[:, half:])
        back[pl.ds(first // cap, nodes_each)] = both.astype(BF)

    def ret_copy(r, to):
        return pltpu.make_async_remote_copy(
            src_ref=back.at[to],
            dst_ref=ret.at[me],
            send_sem=ret_send.at[r],
            recv_sem=ret_recv.at[r],
            device_id={"pts": to},
            device_id_type=MESH,
        )

    @pl.loop(1, nodes)
    def _(r):
        ret_copy(r, lax.rem(me + r, nodes)).start()

    ret[me] = back[me]

    @pl.loop(1, nodes)
    def _(r):
        ret_copy(r, lax.rem(me + r, nodes)).wait_recv()

    ret_rows = nodes * half
    fetch = (iota((rows, ret_rows), 1) == ret_col[:, :1]).astype(F32).astype(BF)
    fetched = dot(fetch, ret[...].reshape(ret_rows, 2 * head_cols))
    lower_row = iota((rows, 2 * head_cols), 0) >= rows // 2
    same = lower_row == (up_col[:, : 2 * head_cols] > 0)
    fetched = jnp.where(same, fetched, pltpu.roll(fetched, head_cols, 1))
    lane_p = iota((rows // 2, 2 * head_cols), 1)
    packed = jnp.where(lane_p < head_cols, fetched[: rows // 2], fetched[rows // 2 :]).astype(BF)
    pack[...] = packed

    def ch_copy(r):
        return pltpu.make_async_remote_copy(
            src_ref=pack,
            dst_ref=gath.at[ch],
            send_sem=ch_send.at[r],
            recv_sem=ch_recv.at[r],
            device_id={"ch": lax.rem(ch + r, chans)},
            device_id_type=MESH,
        )

    for r in range(1, chans):
        ch_copy(r).start()
    gath[ch] = packed

    count = rows // 4
    local = cid_ref[...] - me * count
    own_marks = (iota((count, rows), 0) == local).astype(F32).astype(BF)
    spill_marks = (jnp.broadcast_to(local, (16, rows)) == -1).astype(F32).astype(BF)

    for r in range(1, chans):
        ch_copy(r).wait_recv()

    wide = jnp.concatenate([gath[c] for c in range(chans)], axis=1)
    for part in range(2):
        at = pl.ds(part * (rows // 2), rows // 2)
        out = res[at, :].astype(F32) + dot(wide, pw[part])
        full_ref[at, :] = out.astype(BF)
    lifted = dot(full_ref[...], pool_ref[...])
    width = lifted.shape[1]
    high = lifted.astype(BF)
    rest = (lifted - high.astype(F32)).astype(BF)
    counted = jnp.concatenate([high, jnp.ones((rows, 128), BF)], axis=1)
    spill = dot(spill_marks, counted)
    spill_rest = dot(spill_marks, rest)
    spill_out[:, :width] = (spill[:, :width] + spill_rest)[:8]
    spill_out[:, width:] = spill[:8, width:]

    def spill_copy():
        return pltpu.make_async_remote_copy(
            src_ref=spill_out,
            dst_ref=spill_in,
            send_sem=sp_send,
            recv_sem=sp_recv,
            device_id={"pts": me - 1},
            device_id_type=MESH,
        )

    @pl.when(me > 0)
    def _():
        spill_copy().start()

    @pl.when(me == nodes - 1)
    def _():
        spill_in[...] = jnp.zeros_like(spill_in)

    mine = dot(own_marks, counted)
    sums = mine[:, :width] + dot(own_marks, rest)
    counts = mine[:, width : width + 128]

    @pl.when(me < nodes - 1)
    def _():
        spill_copy().wait_recv()

    last = iota((count, width), 0) == count - 1
    sums = sums + jnp.where(last, spill_in[0:1, :width], 0.0)
    counts = counts[:, :1] + jnp.where(last, spill_in[0:1, width : width + 1], 0.0)
    mean_ref[...] = sums / counts

    @pl.when(me < nodes - 1)
    def _():
        halo_copy(True).wait_send()

    @pl.when(me > 0)
    def _():
        halo_copy(False).wait_send()

    @pl.loop(1, nodes)
    def _(r):
        fwd_copy(r, lax.rem(me + r, nodes)).wait_send()

    @pl.loop(1, nodes)
    def _(r):
        ret_copy(r, lax.rem(me + r, nodes)).wait_send()

    for r in range(1, chans):
        ch_copy(r).wait_send()

    @pl.when(me > 0)
    def _():
        spill_copy().wait_send()


def shards(
    points_in,
    neighbor_offsets,
    kernel_ids,
    cluster_ids,
    owners,
    conv_weight,
    norm_gain,
    norm_bias,
    qkv_weight,
    proj_weight,
    pool_weight,
):
    rows, feats = points_in.shape
    nodes = lax.axis_size("pts")
    chans = lax.axis_size("ch")
    cap = max(2 * rows // nodes, 32)
    width = pool_weight.shape[1]
    head_cols = qkv_weight.shape[2]
    vmem = pl.BlockSpec(memory_space=pltpu.VMEM)
    full, mean = pl.pallas_call(
        functools.partial(kernel, nodes, chans, cap),
        out_shape=(
            jax.ShapeDtypeStruct((rows, feats), BF),
            jax.ShapeDtypeStruct((rows // 4, width), F32),
        ),
        in_specs=[vmem] * 11,
        out_specs=(vmem, vmem),
        scratch_shapes=[
            pltpu.VMEM((rows + 2 * G, feats), BF),
            pltpu.VMEM((128, feats), BF),
            pltpu.VMEM((rows, feats), BF),
            pltpu.VMEM((rows, feats), BF),
            pltpu.VMEM((nodes, cap, feats), BF),
            pltpu.VMEM((nodes, cap, feats), BF),
            pltpu.VMEM((nodes, cap // 2, 2 * head_cols), BF),
            pltpu.VMEM((nodes, cap // 2, 2 * head_cols), BF),
            pltpu.VMEM((rows // 2, 2 * head_cols), BF),
            pltpu.VMEM((chans, rows // 2, 2 * head_cols), BF),
            pltpu.VMEM((2, 2 * feats, feats), BF),
            pltpu.VMEM((8, width + 128), F32),
            pltpu.VMEM((8, width + 128), F32),
            pltpu.SemaphoreType.DMA((2,)),
            pltpu.SemaphoreType.DMA((2,)),
            pltpu.SemaphoreType.DMA((nodes,)),
            pltpu.SemaphoreType.DMA((nodes,)),
            pltpu.SemaphoreType.DMA((nodes,)),
            pltpu.SemaphoreType.DMA((nodes,)),
            pltpu.SemaphoreType.DMA((chans,)),
            pltpu.SemaphoreType.DMA((chans,)),
            pltpu.SemaphoreType.DMA,
            pltpu.SemaphoreType.DMA,
        ],
        compiler_params=pltpu.CompilerParams(
            collective_id=0, has_side_effects=True, vmem_limit_bytes=48 * 1024 * 1024
        ),
    )(
        points_in,
        neighbor_offsets,
        kernel_ids,
        cluster_ids.reshape(1, rows),
        owners.reshape(1, rows),
        conv_weight,
        norm_gain.reshape(1, feats),
        norm_bias.reshape(1, feats),
        qkv_weight,
        proj_weight,
        pool_weight,
    )
    block_out = lax.dynamic_slice_in_dim(full, lax.axis_index("ch") * head_cols, head_cols, 1)
    pooled = jax.nn.gelu(mean, approximate=False).astype(BF)
    return (block_out, pooled)


def solution(mesh):
    return jax.shard_map(
        shards,
        mesh=mesh,
        in_specs=(
            P("pts", None),
            P("pts", None),
            P("pts", None),
            P("pts"),
            P("pts"),
            P(),
            P(),
            P(),
            P(None, None, "ch"),
            P(),
            P(None, "ch"),
        ),
        out_specs=(P("pts", "ch"), P("pts", "ch")),
        check_vma=False,
    )
```

profile of v0, /device:TPU:0, one launch (start us, length us, event | category | flops | bytes accessed | tf_op | source)
XLA Modules:
  0.0 46.1 jit_solution(11150874240900670197)
XLA Ops:
  0.6 0.0 copy-start.9
  0.6 0.0 copy-start.8
  0.7 0.9 %copy.13.off_ref = s32[512,16]{1,0:T(8,128)S(1)} copy(s32[512,16]{0,1:T(8,128)} %param.12) | data formatting | bytes 65536 | tf_op args[1]
  1.6 0.0 copy-done.9
  1.6 0.0 copy-start
  1.6 0.1 copy.14.kid_ref
  1.7 0.0 copy-done.8
  1.7 0.0 copy-start.1
  1.7 0.0 copy-start.2
  1.8 0.0 copy-start.3
  1.8 0.0 copy-start.4
  1.8 0.0 copy-start.5
  1.8 0.0 copy-start.6
  1.8 0.0 copy-start.7
  1.8 0.2 copy.15.qkvw_ref
  2.0 0.6 %copy-done = bf16[512,256]{1,0:T(8,128)(2,1)S(1)} copy-done((bf16[512,256]{1,0:T(8,128)(2,1)S(1)}, bf16[512,256]{1,0:T(8,128)(2,1)}, u32[]{:S(2)}) %copy-start) | copy-done | bytes 262168
  2.5 0.1 copy-done.1
  2.7 0.0 copy-done.2
  2.7 0.0 copy-done.3
  2.7 0.0 copy-done.4
  2.7 0.0 copy-done.5
  2.7 0.0 copy-done.6
  2.7 0.0 copy-done.7
  2.7 41.8 %shard_map.122 = (bf16[512,256]{1,0:T(8,128)(2,1)S(1)}, f32[128,128]{1,0:T(8,128)S(1)}) custom-call(bf16[512,256]{1,0:T(8,128)(2,1)S(1)} %copy-done, s32[512,16]{1,0:T(8,128)S(1)} %copy.13.off_ref, s32[512,16]{1,0:T(8,128)S(1)} %copy.14.kid_ref, s32[1,512]{1,0:T(1,128)S(1)} %bitcast.4, s32[1,512]{1,0:T(1,128)S(1)} %bitcast.5, bf16[27,256]{1,0:T(8,128)(2,1)S(1)} %copy-done.3, ...), custom_call_target="tpu_custom_call" | custom-call | tf_op jit(solution)/shard_map/pallas_call | solution.py:416
  44.5 0.1 constant_dynamic-slice_fusion
  44.6 0.7 %copy.16 = bf16[512,64]{0,1:T(8,128)(2,1)} copy(bf16[512,64]{1,0:T(8,128)(2,1)S(1)} %constant_dynamic-slice_fusion) | data formatting | bytes 131072
  45.3 0.8 %fusion.2 = bf16[128,128]{1,0:T(8,128)(2,1)} fusion(f32[128,128]{1,0:T(8,128)S(1)} %get-tuple-element.5), kind=kLoop, calls=%fused_computation.3 | loop fusion | flops 1064960 | bytes 98304 | tf_op jit(solution)/shard_map/convert_element_type | solution.py:466
Async XLA Ops:
  0.6 0.9 %copy-start.9 = (s32[512,16]{0,1:T(8,128)S(1)}, s32[512,16]{0,1:T(8,128)}, u32[]{:S(2)}) copy-start(s32[512,16]{0,1:T(8,128)} %param.13) | copy-start | bytes 98308
  0.6 1.1 %copy-start.8 = (bf16[3,256,64]{1,2,0:T(8,128)(2,1)S(1)}, bf16[3,256,64]{1,2,0:T(8,128)(2,1)}, u32[]{:S(2)}) copy-start(bf16[3,256,64]{1,2,0:T(8,128)(2,1)} %param.19) | copy-start | bytes 294916
  1.6 1.0 %copy-start = (bf16[512,256]{1,0:T(8,128)(2,1)S(1)}, bf16[512,256]{1,0:T(8,128)(2,1)}, u32[]{:S(2)}) copy-start(bf16[512,256]{1,0:T(8,128)(2,1)} %x_ref.1) | copy-start | bytes 786436
  1.7 0.9 %copy-start.1 = (bf16[256,256]{1,0:T(8,128)(2,1)S(1)}, bf16[256,256]{1,0:T(8,128)(2,1)}, u32[]{:S(2)}) copy-start(bf16[256,256]{1,0:T(8,128)(2,1)} %proj_ref.1) | copy-start | bytes 393220
  1.7 0.9 %copy-start.2 = (bf16[256,128]{1,0:T(8,128)(2,1)S(1)}, bf16[256,128]{1,0:T(8,128)(2,1)}, u32[]{:S(2)}) copy-start(bf16[256,128]{1,0:T(8,128)(2,1)} %pool_ref.1) | copy-start | bytes 196612
  1.8 0.9 %copy-start.3 = (bf16[27,256]{1,0:T(8,128)(2,1)S(1)}, bf16[27,256]{1,0:T(8,128)(2,1)}, u32[]{:S(2)}) copy-start(bf16[27,256]{1,0:T(8,128)(2,1)} %cw_ref.1) | copy-start | bytes 41476
  1.8 0.9 %copy-start.4 = (s32[512]{0:T(512)S(1)}, s32[512]{0:T(512)}, u32[]{:S(2)}) copy-start(s32[512]{0:T(512)} %param.14) | copy-start | bytes 6148
  1.8 0.9 %copy-start.5 = (s32[512]{0:T(512)S(1)}, s32[512]{0:T(512)}, u32[]{:S(2)}) copy-start(s32[512]{0:T(512)} %param.15) | copy-start | bytes 6148
  1.8 0.9 %copy-start.6 = (f32[256]{0:T(256)S(1)}, f32[256]{0:T(256)}, u32[]{:S(2)}) copy-start(f32[256]{0:T(256)} %param.17) | copy-start | bytes 3076
  1.8 0.9 %copy-start.7 = (f32[256]{0:T(256)S(1)}, f32[256]{0:T(256)}, u32[]{:S(2)}) copy-start(f32[256]{0:T(256)} %param.18) | copy-start | bytes 3076
where the time goes:
time: 46.3 us; the launch traced here: 46.1 us
  Pallas kernels  41.8 us (90%)
  local copies, waits for them, and re-layouts  2.76 us (6%)
  between operations  0.79 us (2%)
  other arithmetic  0.77 us (2%)
    pallas_call x1, Pallas kernels, shards(): pl.pallas_call(functools.partial(kernel, nodes, chans, cap), out_shape=(j...  41.8 us
    unnamed x24, local copies, waits for them, and re-layouts  2.66 us

commit v1 on v0

--- a/solution.py
+++ b/solution.py
@@ -24,6 +24,21 @@
 
 def dot(a, b):
     return jnp.dot(a, b, preferred_element_type=F32)
+
+
+def dot_t(a, b):
+    return lax.dot_general(a, b, (((1,), (1,)), ((), ())), preferred_element_type=F32)
+
+
+def each(nodes, count):
+    def run(body):
+        if nodes <= 8:
+            for i in range(count):
+                body(i)
+        else:
+            pl.loop(0, count)(body)
+
+    return run
 
 
 def kernel(
@@ -73,6 +88,7 @@
     half = cap // 2
     slots = nodes * cap
 
+    steps = functools.partial(each, nodes)
     barrier = pltpu.get_barrier_semaphore()
 
     @pl.loop(1, nodes)
@@ -85,6 +101,11 @@
         pl.semaphore_signal(
             barrier, inc=1, device_id={"ch": lax.rem(ch + r, chans)}, device_id_type=MESH
         )
+
+    xp[pl.ds(G, rows), :] = x_ref[...]
+    kinds = cw_ref.shape[0]
+    cw[...] = jnp.zeros_like(cw)
+    cw[pl.ds(0, kinds), :] = cw_ref[...]
     pl.semaphore_wait(barrier, nodes - 1 + chans - 1)
 
     def halo_copy(up):
@@ -117,11 +138,6 @@
     def _():
         xp[pl.ds(rows + G, G), :] = jnp.zeros((G, feats), BF)
 
-    xp[pl.ds(G, rows), :] = x_ref[...]
-    kinds = cw_ref.shape[0]
-    cw[...] = jnp.zeros_like(cw)
-    cw[pl.ds(0, kinds), :] = cw_ref[...]
-
     head_cols = feats // chans
     pw[...] = jnp.zeros_like(pw)
     for c in range(chans):
@@ -144,29 +160,23 @@
     gain = gain_ref[...]
     beta = bias_ref[...]
     wqkv = jnp.concatenate(
-        [
-            qkvw_ref[1],
-            jnp.zeros((feats, head_cols), BF),
-            qkvw_ref[0],
-            qkvw_ref[2],
-        ],
-        axis=1,
+        [qkvw_ref[1], qkvw_ref[0], qkvw_ref[2], jnp.zeros((head_cols, feats), BF)], axis=0
     )
-    ones_lane = jnp.logical_and(
-        iota((TILE, 4 * head_cols), 1) >= head_cols, iota((TILE, 4 * head_cols), 1) < 2 * head_cols
-    )
+    ones_lane = iota((TILE, 4 * head_cols), 1) >= 3 * head_cols
+    offs_all = jnp.transpose(off_ref[...].astype(F32)).astype(jnp.int32)
+    kids_all = jnp.transpose(kid_ref[...].astype(F32)).astype(jnp.int32)
 
     def tile(t):
         base = t * TILE
         window = xp[pl.ds(base, TILE + 2 * G), :]
         weights = cw[...]
-        offs = off_ref[pl.ds(base, TILE), :] + iota((TILE, off_ref.shape[1]), 0) + G
-        kids = kid_ref[pl.ds(base, TILE), :]
+        offs = offs_all[base : base + TILE] + iota((TILE, off_ref.shape[0]), 0) + G
+        kids = kids_all[base : base + TILE]
         lanes = iota((TILE, TILE + 2 * G), 1)
         kind_lanes = iota((TILE, 128), 1)
         conv = x_ref[pl.ds(base, TILE), :].astype(F32)
         total = jnp.zeros((TILE, feats), F32)
-        for first in range(0, off_ref.shape[1], CHUNK):
+        for first in range(0, off_ref.shape[0], CHUNK):
             pick = jnp.concatenate(
                 [
                     (lanes == offs[:, n : n + 1]).astype(F32).astype(BF)
@@ -191,7 +201,7 @@
         centered = features - average
         variance = jnp.mean(centered * centered, axis=1, keepdims=True)
         normed = (centered * lax.rsqrt(variance + 1e-05) * gain + beta).astype(BF)
-        projected = jnp.where(ones_lane, 1.0, dot(normed, wqkv))
+        projected = jnp.where(ones_lane, 1.0, dot_t(normed, wqkv))
         ext[pl.ds(base, TILE), :] = projected.astype(BF)
 
     tiles = rows // TILE
@@ -209,12 +219,6 @@
         halo_copy(False).wait_recv()
 
     tile(tiles - 1)
-
-    rows_each = min(slots, 1024)
-    for first in range(0, slots, rows_each):
-        place = (iota((rows_each, rows), 0) + first == pos_row).astype(F32).astype(BF)
-        placed = dot(place, ext[...]).astype(BF)
-        send[pl.ds(first // cap, rows_each // cap)] = placed.reshape(rows_each // cap, cap, feats)
 
     def fwd_copy(r, to):
         return pltpu.make_async_remote_copy(
@@ -226,50 +230,48 @@
             device_id_type=MESH,
         )
 
-    @pl.loop(1, nodes)
-    def _(r):
-        fwd_copy(r, lax.rem(me + r, nodes)).start()
-
-    recv[me] = send[me]
+    pair = 2 * head_cols
+
+    def block_for(to):
+        place = (iota((cap, rows), 0) + to * cap == pos_row).astype(F32).astype(BF)
+        placed = dot(place, ext[...])
+        lane = iota((cap, pair), 1)
+        dead = jnp.logical_and(lane >= head_cols, placed[:, 3 * head_cols : 3 * head_cols + 1] < 0.5)
+        first = jnp.where(dead, 2.0**100, placed[:, :pair])
+        second = placed[:, pair:]
+        lane_h = iota((half, pair), 1)
+        second = jnp.where(lane_h < head_cols, second[:half], pltpu.roll(second[half:], head_cols, 1))
+        return first.astype(BF), second.astype(BF)
+
+    @steps(nodes - 1)
+    def _(i):
+        to = lax.rem(me + i + 1, nodes)
+        first, second = block_for(to)
+        send[to, pl.ds(0, cap), :] = first
+        send[to, pl.ds(cap, half), :] = second
+        fwd_copy(i + 1, to).start()
+
+    first, second = block_for(me)
+    recv[me, pl.ds(0, cap), :] = first
+    recv[me, pl.ds(cap, half), :] = second
 
     @pl.loop(1, nodes)
     def _(r):
         fwd_copy(r, lax.rem(me + r, nodes)).wait_recv()
 
-    everything = recv[...].reshape(slots, feats)
-    low = everything[:, : 2 * head_cols]
-    lane = iota((slots, 2 * head_cols), 1)
-    keys = jnp.where(
-        lane < head_cols, low.astype(F32), (low.astype(F32) - 1.0) * 1e30
-    ).astype(BF)
-    scale = 1.0 / math.sqrt(HD)
-    nodes_each = QTILE // cap
-    for first in range(0, slots, QTILE):
-        query = recv[pl.ds(first // cap, nodes_each)].reshape(QTILE, feats)[:, 2 * head_cols :]
-        query = query.astype(F32)
-        lane_q = iota((QTILE, 2 * head_cols), 1)
-        answer = jnp.zeros((QTILE, 2 * head_cols), F32)
-        for h in range(head_cols // HD):
-            inside = jnp.logical_and(lane_q >= h * HD, lane_q < (h + 1) * HD)
-            one = jnp.where(lane_q == head_cols, 1.0, 0.0)
-            query_h = jnp.where(inside, query, one).astype(BF)
-            scores = lax.dot_general(
-                query_h, keys, (((1,), (1,)), ((), ())), preferred_element_type=F32
-            )
-            top = jnp.max(scores, axis=1, keepdims=True)
-            soft = jnp.exp((scores - top) * scale).astype(BF)
-            summed = dot(soft, everything)
-            below = summed[:, head_cols : head_cols + 1]
-            below = jnp.where(below == 0.0, 1.0, below)
-            here = jnp.logical_and(
-                lane_q >= head_cols + h * HD, lane_q < head_cols + (h + 1) * HD
-            )
-            answer = jnp.where(here, summed[:, 2 * head_cols :] / below, answer)
-        cube = answer.reshape(nodes_each, cap, 2 * head_cols)
-        moved = pltpu.roll(answer, head_cols, 1).reshape(nodes_each, cap, 2 * head_cols)
-        lane_b = iota((nodes_each, half, 2 * head_cols), 2)
-        both = jnp.where(lane_b < head_cols, moved[:, :half], cube[:, half:])
-        back[pl.ds(first // cap, nodes_each)] = both.astype(BF)
+    big = 1e29
+    low = recv[:, :cap, :].astype(F32).reshape(slots, pair)
+    lane = iota((slots, pair), 1)
+    gone = low > big
+    keys = jnp.where(lane < head_cols, low, jnp.where(gone, -1e30, 0.0)).astype(BF)
+    value = recv[:, cap:, :].astype(F32).reshape(nodes * half, pair)
+    turned = pltpu.roll(value, head_cols, 1).reshape(nodes, half, pair)
+    value = jnp.concatenate([value.reshape(nodes, half, pair), turned], axis=1)
+    alive = jnp.where(gone, 0.0, 1.0)
+    values = jnp.where(lane < head_cols, value.reshape(slots, pair), alive).astype(BF)
+    scale = 1.0 / (math.sqrt(HD) * math.log(2.0))
+    group = QTILE // cap
+    lane_q = iota((QTILE, pair), 1)
 
     def ret_copy(r, to):
         return pltpu.make_async_remote_copy(
@@ -281,11 +283,48 @@
             device_id_type=MESH,
         )
 
-    @pl.loop(1, nodes)
-    def _(r):
-        ret_copy(r, lax.rem(me + r, nodes)).start()
-
-    ret[me] = back[me]
+    @steps(nodes // group)
+    def _(i):
+        whose = [lax.rem(me + i * group + g + 1, nodes) for g in range(group)]
+        query = jnp.concatenate([recv[to, pl.ds(0, cap), :] for to in whose], axis=0).astype(F32)
+        query = pltpu.roll(jnp.where(query > big, 0.0, query), head_cols, 1)
+        answer = jnp.zeros((QTILE, pair), F32)
+        for h in range(head_cols // HD):
+            inside = jnp.logical_and(lane_q >= h * HD, lane_q < (h + 1) * HD)
+            one = jnp.where(lane_q == head_cols, 1.0, 0.0)
+            query_h = jnp.where(inside, query, one).astype(BF)
+            scores = dot_t(query_h, keys)
+            top = jnp.max(scores, axis=1, keepdims=True)
+            soft = jnp.exp2((scores - top) * scale).astype(BF)
+            summed = dot(soft, values)
+            below = summed[:, head_cols : head_cols + 1]
+            below = jnp.where(below == 0.0, 1.0, below)
+            answer = jnp.where(inside, summed / below, answer)
+        moved = pltpu.roll(answer, head_cols, 1)
+        lane_b = iota((half, pair), 1)
+        for g in range(group):
+            at = g * cap
+            both = jnp.where(
+                lane_b < head_cols, answer[at : at + half], moved[at + half : at + cap]
+            ).astype(BF)
+            to = whose[g]
+            r = i * group + g + 1
+            if isinstance(r, int):
+                if r == nodes:
+                    ret[me] = both
+                else:
+                    back[to] = both
+                    ret_copy(r, to).start()
+            else:
+                back[to] = both
+
+                @pl.when(r < nodes)
+                def _():
+                    ret_copy(r, to).start()
+
+                @pl.when(r == nodes)
+                def _():
+                    ret[me] = back[me]
 
     @pl.loop(1, nodes)
     def _(r):
@@ -327,8 +366,9 @@
     for part in range(2):
         at = pl.ds(part * (rows // 2), rows // 2)
         out = res[at, :].astype(F32) + dot(wide, pw[part])
-        full_ref[at, :] = out.astype(BF)
-    lifted = dot(full_ref[...], pool_ref[...])
+        res[at, :] = out.astype(BF)
+    full = res[...]
+    lifted = dot(full, pool_ref[...])
     width = lifted.shape[1]
     high = lifted.astype(BF)
     rest = (lifted - high.astype(F32)).astype(BF)
@@ -356,6 +396,8 @@
     def _():
         spill_in[...] = jnp.zeros_like(spill_in)
 
+    own_lane = iota((head_cols, feats), 1) == iota((head_cols, feats), 0) + ch * head_cols
+    full_ref[...] = dot_t(own_lane.astype(F32).astype(BF), full).astype(BF)
     mine = dot(own_marks, counted)
     sums = mine[:, :width] + dot(own_marks, rest)
     counts = mine[:, width : width + 128]
@@ -416,7 +458,7 @@
     full, mean = pl.pallas_call(
         functools.partial(kernel, nodes, chans, cap),
         out_shape=(
-            jax.ShapeDtypeStruct((rows, feats), BF),
+            jax.ShapeDtypeStruct((head_cols, rows), BF),
             jax.ShapeDtypeStruct((rows // 4, width), F32),
         ),
         in_specs=[vmem] * 11,
@@ -426,8 +468,8 @@
             pltpu.VMEM((128, feats), BF),
             pltpu.VMEM((rows, feats), BF),
             pltpu.VMEM((rows, feats), BF),
-            pltpu.VMEM((nodes, cap, feats), BF),
-            pltpu.VMEM((nodes, cap, feats), BF),
+            pltpu.VMEM((nodes, cap + cap // 2, 2 * head_cols), BF),
+            pltpu.VMEM((nodes, cap + cap // 2, 2 * head_cols), BF),
             pltpu.VMEM((nodes, cap // 2, 2 * head_cols), BF),
             pltpu.VMEM((nodes, cap // 2, 2 * head_cols), BF),
             pltpu.VMEM((rows // 2, 2 * head_cols), BF),
@@ -451,18 +493,18 @@
         ),
     )(
         points_in,
-        neighbor_offsets,
-        kernel_ids,
+        neighbor_offsets.T,
+        kernel_ids.T,
         cluster_ids.reshape(1, rows),
         owners.reshape(1, rows),
         conv_weight,
         norm_gain.reshape(1, feats),
         norm_bias.reshape(1, feats),
-        qkv_weight,
+        jnp.transpose(qkv_weight, (0, 2, 1)),
         proj_weight,
         pool_weight,
     )
-    block_out = lax.dynamic_slice_in_dim(full, lax.axis_index("ch") * head_cols, head_cols, 1)
+    block_out = full.T
     pooled = jax.nn.gelu(mean, approximate=False).astype(BF)
     return (block_out, pooled)
 

time: 46.3 us -> 47 us (1.015)
  local copies, waits for them, and re-layouts: 2.76 us -> 7.14 us
  Pallas kernels: 41.8 us -> 37.9 us
    unnamed x24 -> x23, local copies, waits for them, and re-layouts: 2.66 us -> 7.14 us
    pallas_call x1, Pallas kernels: 41.8 us -> 37.9 us  [shards(): pl.pallas_call(functools.partial(kernel, nodes, chans, cap), out_shape=(j...]
where the time goes in v1:
time: 47 us; the launch traced here: 46.5 us
  Pallas kernels  37.9 us (81%)
  local copies, waits for them, and re-layouts  7.14 us (15%)
  other arithmetic  0.77 us (2%)
  between operations  0.68 us (1%)
    pallas_call x1, Pallas kernels, shards(): pl.pallas_call(functools.partial(kernel, nodes, chans, cap), out_shape=(j...  37.9 us
    unnamed x23, local copies, waits for them, and re-layouts  7.14 us

profile of v1, /device:TPU:0, one launch (start us, length us, event | category | flops | bytes accessed | tf_op | source)
XLA Modules:
  0.0 46.5 jit_solution(2523393394091075998)
XLA Ops:
  0.6 0.0 copy-start.10
  0.6 0.0 copy-start.8
  0.7 0.0 copy-start.7
  0.7 0.0 copy-start.9
  0.7 0.6 %copy-done.10 = f32[256]{0:T(256)S(1)} copy-done((f32[256]{0:T(256)S(1)}, f32[256]{0:T(256)}, u32[]{:S(2)}) %copy-start.10) | copy-done | bytes 1048
  1.3 0.0 copy-done.8
  1.3 0.0 copy-done.7
  1.3 0.0 copy-done.9
  1.4 0.0 copy-start
  1.4 0.9 %copy-done = bf16[512,256]{1,0:T(8,128)(2,1)S(1)} copy-done((bf16[512,256]{1,0:T(8,128)(2,1)S(1)}, bf16[512,256]{1,0:T(8,128)(2,1)}, u32[]{:S(2)}) %copy-start) | copy-done | bytes 262168
  2.3 0.0 copy-start.1
  2.3 0.9 %copy-done.1 = bf16[256,256]{1,0:T(8,128)(2,1)S(1)} copy-done((bf16[256,256]{1,0:T(8,128)(2,1)S(1)}, bf16[256,256]{1,0:T(8,128)(2,1)}, u32[]{:S(2)}) %copy-start.1) | copy-done | bytes 131096
  3.2 0.0 copy-start.2
  3.2 0.9 %copy-done.2 = bf16[3,256,64]{1,2,0:T(8,128)(2,1)S(1)} copy-done((bf16[3,256,64]{1,2,0:T(8,128)(2,1)S(1)}, bf16[3,256,64]{1,2,0:T(8,128)(2,1)}, u32[]{:S(2)}) %copy-start.2) | copy-done | bytes 98328
  4.1 0.0 copy-start.3
  4.1 0.8 %copy-done.3 = bf16[256,128]{1,0:T(8,128)(2,1)S(1)} copy-done((bf16[256,128]{1,0:T(8,128)(2,1)S(1)}, bf16[256,128]{1,0:T(8,128)(2,1)}, u32[]{:S(2)}) %copy-start.3) | copy-done | bytes 65560
  5.0 0.0 copy-start.4
  5.0 0.8 %copy-done.4 = s32[512,16]{0,1:T(8,128)S(1)} copy-done((s32[512,16]{0,1:T(8,128)S(1)}, s32[512,16]{0,1:T(8,128)}, u32[]{:S(2)}) %copy-start.4) | copy-done | bytes 32792
  5.7 0.0 copy-start.5
  5.7 0.8 %copy-done.5 = s32[512,16]{0,1:T(8,128)S(1)} copy-done((s32[512,16]{0,1:T(8,128)S(1)}, s32[512,16]{0,1:T(8,128)}, u32[]{:S(2)}) %copy-start.5) | copy-done | bytes 32792
  6.5 0.0 copy-start.6
  6.5 0.7 %copy-done.6 = bf16[27,256]{1,0:T(8,128)(2,1)S(1)} copy-done((bf16[27,256]{1,0:T(8,128)(2,1)S(1)}, bf16[27,256]{1,0:T(8,128)(2,1)}, u32[]{:S(2)}) %copy-start.6) | copy-done | bytes 13848
  7.2 37.9 %shard_map.122 = (bf16[64,512]{1,0:T(8,128)(2,1)S(1)}, f32[128,128]{1,0:T(8,128)S(1)}) custom-call(bf16[512,256]{1,0:T(8,128)(2,1)S(1)} %copy-done, s32[16,512]{1,0:T(8,128)S(1)} %bitcast.10, s32[16,512]{1,0:T(8,128)S(1)} %bitcast.11, s32[1,512]{1,0:T(1,128)S(1)} %bitcast.12, s32[1,512]{1,0:T(1,128)S(1)} %bitcast.13, bf16[27,256]{1,0:T(8,128)(2,1)S(1)} %copy-done.6, ...), custom_call_target="tpu_custom_call" | custom-call | tf_op jit(solution)/shard_map/pallas_call | solution.py:458
  45.1 0.8 %fusion.2 = bf16[128,128]{1,0:T(8,128)(2,1)} fusion(f32[128,128]{1,0:T(8,128)S(1)} %get-tuple-element.5), kind=kLoop, calls=%fused_computation.3 | loop fusion | flops 1064960 | bytes 98304 | tf_op jit(solution)/shard_map/convert_element_type | solution.py:508
  45.9 0.6 %copy.14 = bf16[512,64]{0,1:T(8,128)(2,1)} copy(bf16[512,64]{0,1:T(8,128)(2,1)S(1)} %bitcast.9) | data formatting | bytes 131072
Async XLA Ops:
  0.6 0.7 %copy-start.10 = (f32[256]{0:T(256)S(1)}, f32[256]{0:T(256)}, u32[]{:S(2)}) copy-start(f32[256]{0:T(256)} %param.18) | copy-start | bytes 3076
  0.6 0.7 %copy-start.8 = (s32[512]{0:T(512)S(1)}, s32[512]{0:T(512)}, u32[]{:S(2)}) copy-start(s32[512]{0:T(512)} %param.15) | copy-start | bytes 6148
  0.7 0.7 %copy-start.7 = (s32[512]{0:T(512)S(1)}, s32[512]{0:T(512)}, u32[]{:S(2)}) copy-start(s32[512]{0:T(512)} %param.14) | copy-start | bytes 6148
  0.7 0.7 %copy-start.9 = (f32[256]{0:T(256)S(1)}, f32[256]{0:T(256)}, u32[]{:S(2)}) copy-start(f32[256]{0:T(256)} %param.17) | copy-start | bytes 3076
  1.4 0.9 %copy-start = (bf16[512,256]{1,0:T(8,128)(2,1)S(1)}, bf16[512,256]{1,0:T(8,128)(2,1)}, u32[]{:S(2)}) copy-start(bf16[512,256]{1,0:T(8,128)(2,1)} %x_ref.1) | copy-start | bytes 786436
  2.3 0.9 %copy-start.1 = (bf16[256,256]{1,0:T(8,128)(2,1)S(1)}, bf16[256,256]{1,0:T(8,128)(2,1)}, u32[]{:S(2)}) copy-start(bf16[256,256]{1,0:T(8,128)(2,1)} %proj_ref.1) | copy-start | bytes 393220
  3.2 0.9 %copy-start.2 = (bf16[3,256,64]{1,2,0:T(8,128)(2,1)S(1)}, bf16[3,256,64]{1,2,0:T(8,128)(2,1)}, u32[]{:S(2)}) copy-start(bf16[3,256,64]{1,2,0:T(8,128)(2,1)} %param.19) | copy-start | bytes 294916
  4.1 0.8 %copy-start.3 = (bf16[256,128]{1,0:T(8,128)(2,1)S(1)}, bf16[256,128]{1,0:T(8,128)(2,1)}, u32[]{:S(2)}) copy-start(bf16[256,128]{1,0:T(8,128)(2,1)} %pool_ref.1) | copy-start | bytes 196612
  5.0 0.8 %copy-start.4 = (s32[512,16]{0,1:T(8,128)S(1)}, s32[512,16]{0,1:T(8,128)}, u32[]{:S(2)}) copy-start(s32[512,16]{0,1:T(8,128)} %param.12) | copy-start | bytes 98308
  5.7 0.8 %copy-start.5 = (s32[512,16]{0,1:T(8,128)S(1)}, s32[512,16]{0,1:T(8,128)}, u32[]{:S(2)}) copy-start(s32[512,16]{0,1:T(8,128)} %param.13) | copy-start | bytes 98308
  6.5 0.7 %copy-start.6 = (bf16[27,256]{1,0:T(8,128)(2,1)S(1)}, bf16[27,256]{1,0:T(8,128)(2,1)}, u32[]{:S(2)}) copy-start(bf16[27,256]{1,0:T(8,128)(2,1)} %cw_ref.1) | copy-start | bytes 41476

commit v2 on v1

--- a/solution.py
+++ b/solution.py
@@ -46,6 +46,18 @@
     chans,
     cap,
     x_ref,
+    off_in,
+    kid_in,
+    cid_in,
+    own_in,
+    cw_in,
+    gain_in,
+    bias_in,
+    qkvw_in,
+    proj_in,
+    pool_in,
+    full_ref,
+    mean_ref,
     off_ref,
     kid_ref,
     cid_ref,
@@ -56,8 +68,7 @@
     qkvw_ref,
     proj_ref,
     pool_ref,
-    full_ref,
-    mean_ref,
+    in_sem,
     xp,
     cw,
     res,
@@ -69,8 +80,9 @@
     pack,
     gath,
     pw,
-    spill_out,
-    spill_in,
+    next_res,
+    next_pack,
+    next_cid,
     halo_send,
     halo_recv,
     fwd_send,
@@ -79,8 +91,10 @@
     ret_recv,
     ch_send,
     ch_recv,
-    sp_send,
-    sp_recv,
+    next_send,
+    next_recv,
+    pack_send,
+    pack_recv,
 ):
     me = lax.axis_index("pts")
     ch = lax.axis_index("ch")
@@ -89,6 +103,26 @@
     slots = nodes * cap
 
     steps = functools.partial(each, nodes)
+    loads = [
+        pltpu.make_async_copy(src, dst, in_sem.at[i])
+        for i, (src, dst) in enumerate(
+            [
+                (own_in, own_ref),
+                (x_ref, xp.at[pl.ds(G, rows)]),
+                (cw_in, cw_ref),
+                (off_in, off_ref),
+                (kid_in, kid_ref),
+                (gain_in, gain_ref),
+                (bias_in, bias_ref),
+                (qkvw_in, qkvw_ref),
+                (proj_in, proj_ref),
+                (pool_in, pool_ref),
+                (cid_in, cid_ref),
+            ]
+        )
+    ]
+    for load in loads:
+        load.start()
     barrier = pltpu.get_barrier_semaphore()
 
     @pl.loop(1, nodes)
@@ -102,11 +136,36 @@
             barrier, inc=1, device_id={"ch": lax.rem(ch + r, chans)}, device_id_type=MESH
         )
 
-    xp[pl.ds(G, rows), :] = x_ref[...]
+    for by in (1, nodes - 1):
+        for r in range(1, chans):
+            beside = {"pts": lax.rem(me + by, nodes), "ch": lax.rem(ch + r, chans)}
+            pl.semaphore_signal(barrier, inc=1, device_id=beside, device_id_type=MESH)
+
     kinds = cw_ref.shape[0]
     cw[...] = jnp.zeros_like(cw)
-    cw[pl.ds(0, kinds), :] = cw_ref[...]
-    pl.semaphore_wait(barrier, nodes - 1 + chans - 1)
+    pw[...] = jnp.zeros_like(pw)
+    pl.semaphore_wait(barrier, nodes - 1 + 3 * (chans - 1))
+
+    def next_copy(at):
+        src, dst = ((cid_in, next_cid), (res.at[pl.ds(0, 16)], next_res))[at]
+        return pltpu.make_async_remote_copy(
+            src_ref=src,
+            dst_ref=dst,
+            send_sem=next_send.at[at],
+            recv_sem=next_recv.at[at],
+            device_id={"pts": me - 1},
+            device_id_type=MESH,
+        )
+
+    def pack_copy(r):
+        return pltpu.make_async_remote_copy(
+            src_ref=pack.at[pl.ds(0, 16)],
+            dst_ref=next_pack.at[ch],
+            send_sem=pack_send.at[r],
+            recv_sem=pack_recv.at[r],
+            device_id={"pts": me - 1, "ch": lax.rem(ch + r, chans)},
+            device_id_type=MESH,
+        )
 
     def halo_copy(up):
         if up:
@@ -129,6 +188,7 @@
     @pl.when(me > 0)
     def _():
         halo_copy(False).start()
+        next_copy(0).start()
 
     @pl.when(me == 0)
     def _():
@@ -137,13 +197,12 @@
     @pl.when(me == nodes - 1)
     def _():
         xp[pl.ds(rows + G, G), :] = jnp.zeros((G, feats), BF)
+        next_res[...] = jnp.zeros_like(next_res)
+        next_pack[...] = jnp.zeros_like(next_pack)
+        next_cid[...] = jnp.full_like(next_cid, -1)
 
     head_cols = feats // chans
-    pw[...] = jnp.zeros_like(pw)
-    for c in range(chans):
-        part = proj_ref[pl.ds(c * head_cols, head_cols), :]
-        pw[0, pl.ds(2 * c * head_cols, head_cols), :] = part
-        pw[1, pl.ds((2 * c + 1) * head_cols, head_cols), :] = part
+    loads[0].wait()
 
     owner_row = own_ref[...]
     owner_rows = max(nodes, 16)
@@ -157,6 +216,9 @@
     ret_col = jnp.transpose(jnp.broadcast_to(ret_row, (128, rows)).astype(F32)).astype(jnp.int32)
     up_col = jnp.transpose(jnp.broadcast_to(upper, (128, rows)).astype(F32)).astype(jnp.int32)
 
+    for load in loads[1:8]:
+        load.wait()
+    cw[pl.ds(0, kinds), :] = cw_ref[...]
     gain = gain_ref[...]
     beta = bias_ref[...]
     wqkv = jnp.concatenate(
@@ -166,27 +228,32 @@
     offs_all = jnp.transpose(off_ref[...].astype(F32)).astype(jnp.int32)
     kids_all = jnp.transpose(kid_ref[...].astype(F32)).astype(jnp.int32)
 
+    one_b = jnp.array(1.0, BF)
+    zero_b = jnp.array(0.0, BF)
+
     def tile(t):
         base = t * TILE
         window = xp[pl.ds(base, TILE + 2 * G), :]
         weights = cw[...]
-        offs = offs_all[base : base + TILE] + iota((TILE, off_ref.shape[0]), 0) + G
-        kids = kids_all[base : base + TILE]
-        lanes = iota((TILE, TILE + 2 * G), 1)
-        kind_lanes = iota((TILE, 128), 1)
-        conv = x_ref[pl.ds(base, TILE), :].astype(F32)
+        middle = TILE // 2
+        offs = offs_all[base : base + TILE] + iota((TILE, off_ref.shape[0]), 0) - middle
+        offs = offs.astype(F32).astype(BF)
+        kids = kids_all[base : base + TILE].astype(F32).astype(BF)
+        lanes = (iota((TILE, TILE + 2 * G), 1) - (G + middle)).astype(F32).astype(BF)
+        kind_lanes = iota((TILE, 128), 1).astype(F32).astype(BF)
+        conv = xp[pl.ds(base + G, TILE), :].astype(F32)
         total = jnp.zeros((TILE, feats), F32)
         for first in range(0, off_ref.shape[0], CHUNK):
             pick = jnp.concatenate(
                 [
-                    (lanes == offs[:, n : n + 1]).astype(F32).astype(BF)
+                    jnp.where(lanes == offs[:, n : n + 1], one_b, zero_b)
                     for n in range(first, first + CHUNK)
                 ],
                 axis=0,
             )
             kind = jnp.concatenate(
                 [
-                    (kind_lanes == kids[:, n : n + 1]).astype(F32).astype(BF)
+                    jnp.where(kind_lanes == kids[:, n : n + 1], one_b, zero_b)
                     for n in range(first, first + CHUNK)
                 ],
                 axis=0,
@@ -214,6 +281,10 @@
 
     tile(0)
 
+    @pl.when(me > 0)
+    def _():
+        next_copy(1).start()
+
     @pl.when(me < nodes - 1)
     def _():
         halo_copy(False).wait_recv()
@@ -250,6 +321,13 @@
         send[to, pl.ds(0, cap), :] = first
         send[to, pl.ds(cap, half), :] = second
         fwd_copy(i + 1, to).start()
+
+    for load in loads[8:]:
+        load.wait()
+    for c in range(chans):
+        part = proj_ref[pl.ds(c * head_cols, head_cols), :]
+        pw[0, pl.ds(2 * c * head_cols, head_cols), :] = part
+        pw[1, pl.ds((2 * c + 1) * head_cols, head_cols), :] = part
 
     first, second = block_for(me)
     recv[me, pl.ds(0, cap), :] = first
@@ -352,12 +430,17 @@
 
     for r in range(1, chans):
         ch_copy(r).start()
+
+    @pl.when(me > 0)
+    def _():
+        for r in range(chans):
+            pack_copy(r).start()
+
     gath[ch] = packed
 
     count = rows // 4
     local = cid_ref[...] - me * count
     own_marks = (iota((count, rows), 0) == local).astype(F32).astype(BF)
-    spill_marks = (jnp.broadcast_to(local, (16, rows)) == -1).astype(F32).astype(BF)
 
     for r in range(1, chans):
         ch_copy(r).wait_recv()
@@ -366,50 +449,35 @@
     for part in range(2):
         at = pl.ds(part * (rows // 2), rows // 2)
         out = res[at, :].astype(F32) + dot(wide, pw[part])
-        res[at, :] = out.astype(BF)
-    full = res[...]
-    lifted = dot(full, pool_ref[...])
-    width = lifted.shape[1]
-    high = lifted.astype(BF)
-    rest = (lifted - high.astype(F32)).astype(BF)
-    counted = jnp.concatenate([high, jnp.ones((rows, 128), BF)], axis=1)
-    spill = dot(spill_marks, counted)
-    spill_rest = dot(spill_marks, rest)
-    spill_out[:, :width] = (spill[:, :width] + spill_rest)[:8]
-    spill_out[:, width:] = spill[:8, width:]
-
-    def spill_copy():
-        return pltpu.make_async_remote_copy(
-            src_ref=spill_out,
-            dst_ref=spill_in,
-            send_sem=sp_send,
-            recv_sem=sp_recv,
-            device_id={"pts": me - 1},
-            device_id_type=MESH,
-        )
-
-    @pl.when(me > 0)
-    def _():
-        spill_copy().start()
-
-    @pl.when(me == nodes - 1)
-    def _():
-        spill_in[...] = jnp.zeros_like(spill_in)
-
+        ext[at, :] = out.astype(BF)
+    full = ext[...]
     own_lane = iota((head_cols, feats), 1) == iota((head_cols, feats), 0) + ch * head_cols
     full_ref[...] = dot_t(own_lane.astype(F32).astype(BF), full).astype(BF)
-    mine = dot(own_marks, counted)
-    sums = mine[:, :width] + dot(own_marks, rest)
-    counts = mine[:, width : width + 128]
+
+    def summed_up(marks, some):
+        lifted = dot(some, pool_ref[...])
+        high = lifted.astype(BF)
+        rest = (lifted - high.astype(F32)).astype(BF)
+        counted = jnp.concatenate([high, jnp.ones((some.shape[0], 128), BF)], axis=1)
+        both = dot(marks, counted)
+        width = lifted.shape[1]
+        return both[:, :width] + dot(marks, rest), both[:, width : width + 1]
+
+    sums, counts = summed_up(own_marks, full)
 
     @pl.when(me < nodes - 1)
     def _():
-        spill_copy().wait_recv()
-
-    last = iota((count, width), 0) == count - 1
-    sums = sums + jnp.where(last, spill_in[0:1, :width], 0.0)
-    counts = counts[:, :1] + jnp.where(last, spill_in[0:1, width : width + 1], 0.0)
-    mean_ref[...] = sums / counts
+        for at in range(2):
+            next_copy(at).wait_recv()
+        for r in range(chans):
+            pack_copy(r).wait_recv()
+
+    next_local = next_cid[...][:, :16] - me * count
+    next_marks = (iota((count, 16), 0) == next_local).astype(F32).astype(BF)
+    next_wide = jnp.concatenate([next_pack[c] for c in range(chans)], axis=1)
+    next_full = (next_res[...].astype(F32) + dot(next_wide, pw[0])).astype(BF)
+    more, more_counts = summed_up(next_marks, next_full)
+    mean_ref[...] = (sums + more) / (counts + more_counts)
 
     @pl.when(me < nodes - 1)
     def _():
@@ -432,7 +500,10 @@
 
     @pl.when(me > 0)
     def _():
-        spill_copy().wait_send()
+        for at in range(2):
+            next_copy(at).wait_send()
+        for r in range(chans):
+            pack_copy(r).wait_send()
 
 
 def shards(
@@ -455,15 +526,28 @@
     width = pool_weight.shape[1]
     head_cols = qkv_weight.shape[2]
     vmem = pl.BlockSpec(memory_space=pltpu.VMEM)
+    hbm = pl.BlockSpec(memory_space=pltpu.HBM)
+    near = pltpu.VMEM
     full, mean = pl.pallas_call(
         functools.partial(kernel, nodes, chans, cap),
         out_shape=(
             jax.ShapeDtypeStruct((head_cols, rows), BF),
             jax.ShapeDtypeStruct((rows // 4, width), F32),
         ),
-        in_specs=[vmem] * 11,
+        in_specs=[hbm] * 11,
         out_specs=(vmem, vmem),
         scratch_shapes=[
+            near(neighbor_offsets.shape[::-1], jnp.int32),
+            near(kernel_ids.shape[::-1], jnp.int32),
+            near((1, rows), jnp.int32),
+            near((1, rows), jnp.int32),
+            near(conv_weight.shape, BF),
+            near((1, feats), F32),
+            near((1, feats), F32),
+            near((3, head_cols, feats), BF),
+            near(proj_weight.shape, BF),
+            near(pool_weight.shape, BF),
+            pltpu.SemaphoreType.DMA((11,)),
             pltpu.VMEM((rows + 2 * G, feats), BF),
             pltpu.VMEM((128, feats), BF),
             pltpu.VMEM((rows, feats), BF),
@@ -475,8 +559,9 @@
             pltpu.VMEM((rows // 2, 2 * head_cols), BF),
             pltpu.VMEM((chans, rows // 2, 2 * head_cols), BF),
             pltpu.VMEM((2, 2 * feats, feats), BF),
-            pltpu.VMEM((8, width + 128), F32),
-            pltpu.VMEM((8, width + 128), F32),
+            pltpu.VMEM((16, feats), BF),
+            pltpu.VMEM((chans, 16, 2 * head_cols), BF),
+            pltpu.VMEM((1, rows), jnp.int32),
             pltpu.SemaphoreType.DMA((2,)),
             pltpu.SemaphoreType.DMA((2,)),
             pltpu.SemaphoreType.DMA((nodes,)),
@@ -485,11 +570,13 @@
             pltpu.SemaphoreType.DMA((nodes,)),
             pltpu.SemaphoreType.DMA((chans,)),
             pltpu.SemaphoreType.DMA((chans,)),
-            pltpu.SemaphoreType.DMA,
-            pltpu.SemaphoreType.DMA,
+            pltpu.SemaphoreType.DMA((2,)),
+            pltpu.SemaphoreType.DMA((2,)),
+            pltpu.SemaphoreType.DMA((chans,)),
+            pltpu.SemaphoreType.DMA((chans,)),
         ],
         compiler_params=pltpu.CompilerParams(
-            collective_id=0, has_side_effects=True, vmem_limit_bytes=48 * 1024 * 1024
+            collective_id=0, has_side_effects=True, vmem_limit_bytes=64 * 1024 * 1024
         ),
     )(
         points_in,

time: 47 us -> 40.4 us (0.86)
  local copies, waits for them, and re-layouts: 7.14 us -> 0.63 us
  other arithmetic: 0.77 us -> 1.64 us
  Pallas kernels: 37.9 us -> 37.3 us
    unnamed x23 -> x3, local copies, waits for them, and re-layouts: 7.14 us -> 0.63 us
    convert_element_type x1, other arithmetic: 0.77 us -> 1.64 us  [shards(): pooled = jax.nn.gelu(mean, approximate=False).astype(BF)]
    pallas_call x1, Pallas kernels: 37.9 us -> 37.3 us  [shards(): pl.pallas_call(functools.partial(kernel, nodes, chans, cap), out_shape=(j...]
where the time goes in v2:
time: 40.4 us; the launch traced here: 40.2 us
  Pallas kernels  37.3 us (92%)
  other arithmetic  1.64 us (4%)
  between operations  0.65 us (2%)
  local copies, waits for them, and re-layouts  0.63 us (2%)
    pallas_call x1, Pallas kernels, shards(): pl.pallas_call(functools.partial(kernel, nodes, chans, cap), out_shape=(j...  37.3 us
    convert_element_type x1, other arithmetic, shards(): pooled = jax.nn.gelu(mean, approximate=False).astype(BF)  1.64 us

profile of v2, /device:TPU:0, one launch (start us, length us, event | category | flops | bytes accessed | tf_op | source)
XLA Modules:
  0.0 40.2 jit_solution(14610732684588373381)
XLA Ops:
  0.6 37.3 %shard_map.122 = (bf16[64,512]{1,0:T(8,128)(2,1)}, f32[128,128]{1,0:T(8,128)}) custom-call(bf16[512,256]{1,0:T(8,128)(2,1)} %x_ref.1, s32[16,512]{1,0:T(8,128)} %bitcast.10, s32[16,512]{1,0:T(8,128)} %bitcast.11, s32[1,512]{1,0:T(1,128)} %bitcast.12, s32[1,512]{1,0:T(1,128)} %bitcast.13, bf16[27,256]{1,0:T(8,128)(2,1)} %cw_in.1, f32[1,256]{1,0:T(1,128)} %bitcast.14, ...), custom_call_target="tpu_custom_call" | custom-call | tf_op jit(solution)/shard_map/pallas_call | solution.py:531
  38.0 0.0 copy-start
  38.0 1.6 %fusion.2 = bf16[128,128]{1,0:T(8,128)(2,1)} fusion(f32[128,128]{1,0:T(8,128)} %get-tuple-element.5), kind=kLoop, calls=%fused_computation.3 | loop fusion | flops 1064960 | bytes 98304 | tf_op jit(solution)/shard_map/convert_element_type | solution.py:595
  39.6 0.0 copy-done
  39.6 0.6 %copy.14 = bf16[512,64]{0,1:T(8,128)(2,1)} copy(bf16[512,64]{0,1:T(8,128)(2,1)S(1)} %bitcast.9) | data formatting | bytes 131072
Async XLA Ops:
  38.0 1.7 %copy-start = (bf16[64,512]{1,0:T(8,128)(2,1)S(1)}, bf16[64,512]{1,0:T(8,128)(2,1)}, u32[]{:S(2)}) copy-start(bf16[64,512]{1,0:T(8,128)(2,1)} %get-tuple-element.4) | copy-start | bytes 196612

commit v3 on v2

--- a/solution.py
+++ b/solution.py
@@ -56,8 +56,11 @@
     qkvw_in,
     proj_in,
     pool_in,
+    full_out,
+    pooled_out,
     full_ref,
-    mean_ref,
+    pooled_ref,
+    out_sem,
     off_ref,
     kid_ref,
     cid_ref,
@@ -103,6 +106,11 @@
     slots = nodes * cap
 
     steps = functools.partial(each, nodes)
+    far = sorted(range(1, nodes), key=lambda r: abs(2 * r - nodes)) + [nodes]
+
+    def distance(i):
+        return far[i] if isinstance(i, int) else i + 1
+
     loads = [
         pltpu.make_async_copy(src, dst, in_sem.at[i])
         for i, (src, dst) in enumerate(
@@ -316,11 +324,12 @@
 
     @steps(nodes - 1)
     def _(i):
-        to = lax.rem(me + i + 1, nodes)
+        r = distance(i)
+        to = lax.rem(me + r, nodes)
         first, second = block_for(to)
         send[to, pl.ds(0, cap), :] = first
         send[to, pl.ds(cap, half), :] = second
-        fwd_copy(i + 1, to).start()
+        fwd_copy(r, to).start()
 
     for load in loads[8:]:
         load.wait()
@@ -363,7 +372,7 @@
 
     @steps(nodes // group)
     def _(i):
-        whose = [lax.rem(me + i * group + g + 1, nodes) for g in range(group)]
+        whose = [lax.rem(me + distance(i * group + g), nodes) for g in range(group)]
         query = jnp.concatenate([recv[to, pl.ds(0, cap), :] for to in whose], axis=0).astype(F32)
         query = pltpu.roll(jnp.where(query > big, 0.0, query), head_cols, 1)
         answer = jnp.zeros((QTILE, pair), F32)
@@ -386,7 +395,7 @@
                 lane_b < head_cols, answer[at : at + half], moved[at + half : at + cap]
             ).astype(BF)
             to = whose[g]
-            r = i * group + g + 1
+            r = distance(i * group + g)
             if isinstance(r, int):
                 if r == nodes:
                     ret[me] = both
@@ -453,6 +462,8 @@
     full = ext[...]
     own_lane = iota((head_cols, feats), 1) == iota((head_cols, feats), 0) + ch * head_cols
     full_ref[...] = dot_t(own_lane.astype(F32).astype(BF), full).astype(BF)
+    full_copy = pltpu.make_async_copy(full_ref, full_out, out_sem.at[0])
+    full_copy.start()
 
     def summed_up(marks, some):
         lifted = dot(some, pool_ref[...])
@@ -477,7 +488,13 @@
     next_wide = jnp.concatenate([next_pack[c] for c in range(chans)], axis=1)
     next_full = (next_res[...].astype(F32) + dot(next_wide, pw[0])).astype(BF)
     more, more_counts = summed_up(next_marks, next_full)
-    mean_ref[...] = (sums + more) / (counts + more_counts)
+    mean = (sums + more) / (counts + more_counts)
+    pooled_ref[...] = (mean * (1.0 + lax.erf(mean * math.sqrt(0.5))) * 0.5).astype(BF)
+    pooled_copy = pltpu.make_async_copy(pooled_ref, pooled_out, out_sem.at[1])
+    pooled_copy.start()
+
+    full_copy.wait()
+    pooled_copy.wait()
 
     @pl.when(me < nodes - 1)
     def _():
@@ -525,18 +542,20 @@
     cap = max(2 * rows // nodes, 32)
     width = pool_weight.shape[1]
     head_cols = qkv_weight.shape[2]
-    vmem = pl.BlockSpec(memory_space=pltpu.VMEM)
     hbm = pl.BlockSpec(memory_space=pltpu.HBM)
     near = pltpu.VMEM
-    full, mean = pl.pallas_call(
+    full, pooled = pl.pallas_call(
         functools.partial(kernel, nodes, chans, cap),
         out_shape=(
             jax.ShapeDtypeStruct((head_cols, rows), BF),
-            jax.ShapeDtypeStruct((rows // 4, width), F32),
+            jax.ShapeDtypeStruct((rows // 4, width), BF),
         ),
         in_specs=[hbm] * 11,
-        out_specs=(vmem, vmem),
+        out_specs=(hbm, hbm),
         scratch_shapes=[
+            near((head_cols, rows), BF),
+            near((rows // 4, width), BF),
+            pltpu.SemaphoreType.DMA((2,)),
             near(neighbor_offsets.shape[::-1], jnp.int32),
             near(kernel_ids.shape[::-1], jnp.int32),
             near((1, rows), jnp.int32),
@@ -592,7 +611,6 @@
         pool_weight,
     )
     block_out = full.T
-    pooled = jax.nn.gelu(mean, approximate=False).astype(BF)
     return (block_out, pooled)
 
 

time: 40.4 us -> 40.3 us (level)
  other arithmetic: 1.64 us -> 0 us
  local copies, waits for them, and re-layouts: 0.63 us -> 2.1 us
    convert_element_type x1 -> x0, other arithmetic: 1.64 us -> none  [shards(): pooled = jax.nn.gelu(mean, approximate=False).astype(BF)]
    unnamed x3 -> x4, local copies, waits for them, and re-layouts: 0.63 us -> 2.1 us
where the time goes in v3:
time: 40.3 us; the launch traced here: 40.2 us
  Pallas kernels  37.4 us (93%)
  local copies, waits for them, and re-layouts  2.1 us (5%)
  between operations  0.65 us (2%)
    pallas_call x1, Pallas kernels, shards(): pl.pallas_call(functools.partial(kernel, nodes, chans, cap), out_shape=(j...  37.4 us
    unnamed x4, local copies, waits for them, and re-layouts  2.1 us

profile of v3, /device:TPU:0, one launch (start us, length us, event | category | flops | bytes accessed | tf_op | source)
XLA Modules:
  0.0 40.2 jit_solution(12594421716610085137)
XLA Ops:
  0.6 37.4 %shard_map.122 = (bf16[64,512]{1,0:T(8,128)(2,1)}, bf16[128,128]{1,0:T(8,128)(2,1)}) custom-call(bf16[512,256]{1,0:T(8,128)(2,1)} %x_ref.1, s32[16,512]{1,0:T(8,128)} %bitcast.10, s32[16,512]{1,0:T(8,128)} %bitcast.11, s32[1,512]{1,0:T(1,128)} %bitcast.12, s32[1,512]{1,0:T(1,128)} %bitcast.13, bf16[27,256]{1,0:T(8,128)(2,1)} %cw_in.1, f32[1,256]{1,0:T(1,128)} %bitcast.14, ...), custom_call_target="tpu_custom_call" | custom-call | tf_op jit(solution)/shard_map/pallas_call | solution.py:547
  38.1 0.0 copy-start
  38.1 1.5 %copy.15 = bf16[512,64]{0,1:T(8,128)(2,1)} copy(bf16[512,64]{0,1:T(8,128)(2,1)} %bitcast.9) | data formatting | bytes 131072
  39.6 0.0 copy-done
  39.6 0.6 %copy.16 = bf16[128,128]{1,0:T(8,128)(2,1)} copy(bf16[128,128]{1,0:T(8,128)(2,1)S(1)} %copy-done) | data formatting | bytes 65536
Async XLA Ops:
  38.1 1.5 %copy-start = (bf16[128,128]{1,0:T(8,128)(2,1)S(1)}, bf16[128,128]{1,0:T(8,128)(2,1)}, u32[]{:S(2)}) copy-start(bf16[128,128]{1,0:T(8,128)(2,1)} %get-tuple-element.9) | copy-start | bytes 98308
